TPU v7x, 32 devices: a whole 2x2x4 slice. The times are simulated.
32 devices in a mesh: ctx: 16 (over z, x, core), head: 2 (over y).
Axes of the slice: x: 2, y: 2, z: 4, core: 2. Of those that a mesh axis runs over, the one named last changes fastest.
Arguments:
- queries: bfloat16 [4096, 2048], P('ctx', 'head'), may hold values from -40 to 40
- keys: bfloat16 [4096, 2048], P('ctx', 'head'), may hold values from -4 to 4
- values: bfloat16 [4096, 2048], P('ctx', 'head'), may hold values from -5 to 5
- selected: int32 [16, 128, 3], P('head', 'ctx'), may hold values from 0 to 15, as said below
- out_weight: bfloat16 [2048, 2048], P(None, 'head'), may hold values from -0.125 to 0.125
Outputs:
- projected: bfloat16 [4096, 2048], P('ctx', 'head')
Inputs may be any that keep to these rules, and one draw needn't show every extreme that they name: `selected`: entry 0 of a tile's selection is its own block; entries 1 and 2 are two different earlier blocks, or both the own block where no earlier block is chosen for the tile (one earlier block and the own block in the second key block). For each head, the tiles of one key block name any one other block at most 2 times, and exactly 2 times for every block they name, from the third key block on.
All inputs are finite; a program needn't handle non-finite values.
Results may differ from a plain program's by a relative error of at most 0.0054.
Values may be sent and summed in bfloat16 or wider, within the bound.
A program may use at most 64 MiB of HBM per device.

v0:
```python
import math

import jax
import jax.numpy as jnp
from jax import lax
from jax.sharding import PartitionSpec as P

CAP = 2


def owner_block(group, keys_three, vals_three, scale):
    scores = (
        jnp.einsum("gchtd,khd->gchtk", group, keys_three, preferred_element_type=jnp.float32)
        * scale
    )
    top = jnp.max(scores, axis=-1)
    prob = jnp.exp(scores - top[..., None])
    total = jnp.sum(prob, axis=-1)
    part = jnp.einsum(
        "gchtk,khd->gchtd",
        prob.astype(jnp.bfloat16),
        vals_three,
        preferred_element_type=jnp.float32,
    )
    return (part / total[..., None], top + jnp.log(total))


def partials_back(outputs, sums):
    return (
        lax.all_to_all(outputs, "ctx", split_axis=0, concat_axis=0, tiled=True),
        lax.all_to_all(sums, "ctx", split_axis=0, concat_axis=0, tiled=True),
    )


def group_size(sources, rows_each):
    size = max(1, 512 // rows_each)
    size = min(size, sources)
    while sources % size != 0:
        size = size - 1
    return size


def local(queries, keys, values, selected, out_weight):
    heads_loc = selected.shape[0]
    tiles = selected.shape[1]
    tokens_here = queries.shape[0]
    width = queries.shape[1] // heads_loc
    tile_rows = tokens_here // tiles
    sources = lax.axis_size("ctx")
    mine = lax.axis_index("ctx")
    scale = width ** (-0.5)
    quer_three = queries.reshape(tokens_here, heads_loc, width)
    keys_three = keys.reshape(tokens_here, heads_loc, width)
    vals_three = values.reshape(tokens_here, heads_loc, width)
    rows_blk = math.gcd(tokens_here, 512)
    row_groups = tokens_here // rows_blk
    key_pos = jnp.arange(tokens_here, dtype=jnp.int32)

    def own_rows(args):
        query_rows, start = args
        scores = (
            jnp.einsum("rhd,khd->hrk", query_rows, keys_three, preferred_element_type=jnp.float32)
            * scale
        )
        allowed = (start + jnp.arange(rows_blk, dtype=jnp.int32))[:, None] >= key_pos[None, :]
        scores = jnp.where(allowed[None], scores, jnp.float32(-1e30))
        top = jnp.max(scores, axis=-1)
        prob = jnp.exp(scores - top[..., None])
        total = jnp.sum(prob, axis=-1)
        part = jnp.einsum(
            "hrk,khd->hrd",
            prob.astype(jnp.bfloat16),
            vals_three,
            preferred_element_type=jnp.float32,
        )
        return (part / total[..., None], top + jnp.log(total))

    own_out, own_lse = lax.map(
        own_rows,
        (
            quer_three.reshape(row_groups, rows_blk, heads_loc, width),
            jnp.arange(row_groups, dtype=jnp.int32) * rows_blk,
        ),
    )
    own_out = jnp.transpose(own_out, (1, 0, 2, 3)).reshape(heads_loc, tiles, tile_rows, width)
    own_lse = jnp.transpose(own_lse, (1, 0, 2)).reshape(heads_loc, tiles, tile_rows)
    picks = selected[:, :, 1:]
    valid = picks != mine
    target = jnp.where(valid, picks, sources)
    onehot = (target[..., None] == jnp.arange(sources, dtype=jnp.int32)).astype(jnp.int32)
    flat_hot = onehot.reshape(heads_loc, tiles * 2, sources)
    before = jnp.cumsum(flat_hot, axis=1) - flat_hot
    slot = jnp.sum(before * flat_hot, axis=-1).reshape(heads_loc, tiles, 2)
    head_idx = jnp.broadcast_to(
        jnp.arange(heads_loc, dtype=jnp.int32)[:, None, None], (heads_loc, tiles, 2)
    )
    query_src = jnp.transpose(quer_three.reshape(tiles, tile_rows, heads_loc, width), (2, 0, 1, 3))
    query_pairs = jnp.broadcast_to(query_src[:, :, None], (heads_loc, tiles, 2, tile_rows, width))
    send_q = jnp.zeros((sources, CAP, heads_loc, tile_rows, width), jnp.bfloat16)
    send_q = send_q.at[target, slot, head_idx].set(query_pairs, mode="drop")
    got_rows = lax.all_to_all(send_q, "ctx", split_axis=0, concat_axis=0, tiled=True)
    count = got_rows.shape[1]
    group_count = group_size(sources, count * heads_loc * tile_rows)
    query_groups = got_rows.reshape(
        sources // group_count, group_count, count, heads_loc, tile_rows, width
    )

    def one_group(group):
        return owner_block(group, keys_three, vals_three, scale)

    outputs, sums = lax.map(one_group, query_groups)
    got_out, got_lse = partials_back(
        outputs.reshape(sources, count, heads_loc, tile_rows, width),
        sums.reshape(sources, count, heads_loc, tile_rows),
    )
    clipped = jnp.clip(target, 0, sources - 1)
    pick_out = got_out[clipped, slot, head_idx]
    pick_lse = got_lse[clipped, slot, head_idx]
    keep = valid[..., None]
    top = jnp.maximum(own_lse, jnp.max(jnp.where(keep, pick_lse, own_lse[:, :, None]), axis=2))
    own_w = jnp.exp(own_lse - top)
    pick_w = jnp.exp(jnp.where(keep, pick_lse - top[:, :, None], jnp.float32(-1e30)))
    numer = own_w[..., None] * own_out + jnp.sum(pick_w[..., None] * pick_out, axis=2)
    denom = own_w + jnp.sum(pick_w, axis=2)
    attention = jnp.transpose(numer / denom[..., None], (1, 2, 0, 3)).reshape(
        tokens_here, heads_loc * width
    )
    attention = attention.astype(jnp.bfloat16)
    projected = jnp.dot(
        lax.all_gather(attention, "head", axis=1, tiled=True),
        out_weight,
        preferred_element_type=jnp.float32,
    )
    return projected.astype(jnp.bfloat16)


def solution(mesh):
    return jax.shard_map(
        local,
        mesh=mesh,
        in_specs=(
            P("ctx", "head"),
            P("ctx", "head"),
            P("ctx", "head"),
            P("head", "ctx", None),
            P(None, "head"),
        ),
        out_specs=P("ctx", "head"),
        check_vma=False,
    )
```

profile of v0, /device:TPU:16, one launch (start us, length us, event | category | flops | bytes accessed | tf_op | source)
XLA Modules:
  0.0 272.0 jit_solution(6316098805300373104)
XLA Ops:
  6.5 0.7 slice_select_fusion
  7.3 0.4 fusion.43
  8.1 1.1 copy.70
  9.6 1.8 broadcast_in_dim.120
  11.4 14.8 %scatter_fusion = bf16[16,2,8,32,128]{4,3,2,1,0:T(8,128)(2,1)} fusion(bf16[16,2,8,32,128]{4,3,2,1,0:T(8,128)(2,1)} %broadcast_in_dim.120, s32[128]{0:T(128)S(1)} %reshape.192, bf16[128,32,128]{2,1,0:T(8,128)(2,1)S(1)} %bitcast.117), kind=kCustom, calls=%fused_computation.2 | custom fusion | bytes 3147264 | tf_op jit(solution)/shard_map/scatter | solution.py:100
  26.2 6.3 %all-to-all-start = ((bf16[16,2,8,32,128]{4,3,2,1,0:T(8,128)(2,1)}), bf16[16,2,8,32,128]{4,3,2,1,0:T(8,128)(2,1)S(1)}, u32[]{:S(2)}, u32[]{:S(2)}) async-start(bf16[16,2,8,32,128]{4,3,2,1,0:T(8,128)(2,1)} %scatter_fusion), calls=%async_computation | async-start | bytes 4194304 | tf_op jit(solution)/shard_map/all_to_all | solution.py:101
  33.0 2.0 copy.49
  35.1 2.1 copy.52
  37.1 43.0 %all-to-all-done = bf16[16,2,8,32,128]{4,3,2,1,0:T(8,128)(2,1)S(1)} async-done(((bf16[16,2,8,32,128]{4,3,2,1,0:T(8,128)(2,1)}), bf16[16,2,8,32,128]{4,3,2,1,0:T(8,128)(2,1)S(1)}, u32[]{:S(2)}, u32[]{:S(2)}) %all-to-all-start) | async-done | bytes 2097184 | tf_op jit(solution)/shard_map/all_to_all | solution.py:101
  80.1 44.5 %while.2 = (s32[]{:T(128)}, f32[16,1,2,8,32,128]{5,4,2,3,1,0:T(8,128)}, f32[16,1,2,8,32]{4,3,2,0,1:T(8,128)S(1)}, bf16[16,1,2,8,32,128]{5,4,3,2,0,1:T(8,128)(2,1...) while((s32[]{:T(128)}, f32[16,1,2,8,32,128]{5,4,2,3,1,0:T(8,128)}, ...), condition=%wide.region_8.9_spmd, body=%wide.region_5.8_spmd.sunk | while | flops 67960320 | bytes 3047521 | solution.py:111
  80.1 0.4 fusion.56
  80.5 0.3 fusion.57
  80.8 2.0 fusion.58
  82.9 0.4 fusion.56
  83.3 0.3 fusion.57
  83.6 2.0 fusion.58
  85.7 0.4 fusion.56
  86.1 0.3 fusion.57
  86.4 2.0 fusion.58
  88.5 0.4 fusion.56
  88.9 0.3 fusion.57
  89.1 2.1 fusion.58
  91.2 0.4 fusion.56
  91.9 2.1 fusion.58
  94.0 0.4 fusion.56
  94.7 2.1 fusion.58
  96.8 0.4 fusion.56
  97.5 2.1 fusion.58
  99.6 0.4 fusion.56
  100.3 2.1 fusion.58
  102.4 0.4 fusion.56
  103.1 2.1 fusion.58
  105.2 0.4 fusion.56
  105.9 2.0 fusion.58
  108.0 0.4 fusion.56
  108.7 2.1 fusion.58
  110.8 0.4 fusion.56
  111.4 2.1 fusion.58
  113.6 0.4 fusion.56
  114.2 2.1 fusion.58
  116.3 0.4 fusion.56
  117.0 2.1 fusion.58
  119.1 0.4 fusion.56
  119.8 2.0 fusion.58
  121.9 0.4 fusion.56
  122.6 2.1 fusion.58
  124.8 8.7 %all_to_all.15 = f32[16,1,512]{2,1,0:T(1,128)S(1)} all-to-all(f32[16,1,512]{2,1,0:T(1,128)S(1)} %reshape.205), channel_id=1, replica_groups=mesh['ctx'=16,'head'=2] {'ctx'}, dimensions={0} | all-to-all | bytes 65536 | tf_op jit(solution)/shard_map/all_to_all | solution.py:31
  133.5 7.0 %all-to-all-start.2 = ((f32[16,2,8,32,128]{4,3,1,2,0:T(8,128)}), f32[16,2,8,32,128]{4,3,1,2,0:T(8,128)}, u32[]{:S(2)}, u32[]{:S(2)}) async-start(f32[16,2,8,32,128]{4,3,1,2,0:T(8,128)} %bitcast.118), calls=%async_computation.2 | async-start | bytes 8388608 | tf_op jit(solution)/shard_map/all_to_all | solution.py:30
  140.8 0.6 fusion.11
  141.4 0.4 fusion.13
  142.1 0.4 copy-done.1
  142.4 2.0 convolution_divide_fusion
  144.4 0.5 broadcast.175
  144.9 0.7 reduce.2
  145.7 1.2 gather_fusion
  147.3 85.8 %all-to-all-done.2 = f32[16,2,8,32,128]{4,3,1,2,0:T(8,128)} async-done(((f32[16,2,8,32,128]{4,3,1,2,0:T(8,128)}), f32[16,2,8,32,128]{4,3,1,2,0:T(8,128)}, u32[]{:S(2)}, u32[]{:S(2)}) %all-to-all-start.2) | async-done | bytes 4194336 | tf_op jit(solution)/shard_map/all_to_all | solution.py:30
  233.1 3.2 %gather_fusion.1 = f32[128,32,128]{2,1,0:T(8,128)S(1)} fusion(f32[16,2,8,32,128]{4,3,1,2,0:T(8,128)} %all-to-all-done.2, s32[128]{0:T(128)S(1)} %reshape.180), kind=kCustom, calls=%fused_computation.1 | custom fusion | bytes 4195840 | tf_op jit(solution)/shard_map/gather | solution.py:117
  236.3 0.9 multiply_reduce_fusion
  237.2 0.3 copy-done.2
  237.5 0.7 fusion.23
  238.3 0.3 copy.57
  238.6 0.9 copy.84
  239.5 21.1 %all-gather.2.cloned.1.call-done = bf16[256,2048]{1,0:T(8,128)(2,1)} async-done(((bf16[256,1024]{1,0:T(8,128)(2,1)}), bf16[256,2048]{1,0:T(8,128)(2,1)}) %all-gather.2.cloned.1.call-update) | async-done | bytes 1048592 | tf_op jit(solution)/shard_map/all_gather | solution.py:130
  260.6 4.6 %convolution_convert_fusion = bf16[256,1024]{1,0:T(8,128)(2,1)} fusion(bf16[256,2048]{1,0:T(8,128)(2,1)} %all-gather.2.cloned.1.call-done, bf16[2048,1024]{1,0:T(8,128)(2,1)} %param.11), kind=kOutput, calls=%fused_computation.27 | convolution fusion | flops 1074003968 | bytes 5767168 | tf_op jit(solution)/shard_map/dot_general | solution.py:129
  (76 shorter events, 6.1 us)
Async XLA Ops:
  26.2 6.3 %copy-start.3 = (bf16[256,1024]{1,0:T(8,128)(2,1)S(1)}, bf16[256,1024]{1,0:T(8,128)(2,1)}, u32[]{:S(2)}) copy-start(bf16[256,1024]{1,0:T(8,128)(2,1)} %param.8) | copy-start | bytes 1572868
  26.2 53.9 %all-to-all-start = ((bf16[16,2,8,32,128]{4,3,2,1,0:T(8,128)(2,1)}), bf16[16,2,8,32,128]{4,3,2,1,0:T(8,128)(2,1)S(1)}, u32[]{:S(2)}, u32[]{:S(2)}) async-start(bf16[16,2,8,32,128]{4,3,2,1,0:T(8,128)(2,1)} %scatter_fusion), calls=%async_computation | async-start | bytes 4194304 | tf_op jit(solution)/shard_map/all_to_all | solution.py:101
  133.5 7.3 %copy-start = (bf16[256,1024]{1,0:T(8,128)(2,1)S(1)}, bf16[256,1024]{1,0:T(8,128)(2,1)}, u32[]{:S(2)}) copy-start(bf16[256,1024]{1,0:T(8,128)(2,1)} %param.7) | copy-start | bytes 1572868
  133.5 99.7 %all-to-all-start.2 = ((f32[16,2,8,32,128]{4,3,1,2,0:T(8,128)}), f32[16,2,8,32,128]{4,3,1,2,0:T(8,128)}, u32[]{:S(2)}, u32[]{:S(2)}) async-start(f32[16,2,8,32,128]{4,3,1,2,0:T(8,128)} %bitcast.118), calls=%async_computation.2 | async-start | bytes 8388608 | tf_op jit(solution)/shard_map/all_to_all | solution.py:30
  140.4 120.1 %all-gather.2.cloned.1.call-start = ((), (), s32[]{:S(2)}) async-start(), calls=%async_computation.3 | async-start | bytes 1572864 | tf_op jit(solution)/shard_map/all_gather | solution.py:130
  141.4 1.0 copy-start.1
  236.3 1.2 copy-start.2
Sparse Core Ops, SparseCore 0:
  239.6 20.8 all-gather.1
where the time goes:
time: 276 us; the launch traced here: 272 us
  waiting for transfers between devices  150 us (54%)
  matrix products  46.3 us (17%)
  local copies, waits for them, and re-layouts  30.7 us (11%)
  between operations  13.6 us (5%)
  starting transfers between devices  13.3 us (5%)
  other arithmetic  9.04 us (3%)
  blocking collectives  8.67 us (3%)
    all_to_all x1, waiting for transfers between devices, partials_back(): lax.all_to_all(outputs, 'ctx', split_axis=0, concat_axis=0, tiled=True)  85.8 us
    all_to_all x1, waiting for transfers between devices, local(): lax.all_to_all(send_q, 'ctx', split_axis=0, concat_axis=0, tiled=True)  43 us
    dot_general x16, matrix products, owner_block(): jnp.einsum('gchtk,khd->gchtd', prob.astype(jnp.bfloat16), vals_three, pre...  32.9 us
    all_gather x1, waiting for transfers between devices, local(): lax.all_gather(attention, 'head', axis=1, tiled=True)  21.1 us
    scatter x1, local copies, waits for them, and re-layouts, local(): send_q = send_q.at[target, slot, head_idx].set(query_pairs, mode='drop')  14.8 us
    all_to_all x1, blocking collectives, partials_back(): lax.all_to_all(sums, 'ctx', split_axis=0, concat_axis=0, tiled=True)  8.67 us
    all_to_all x1, starting transfers between devices, partials_back(): lax.all_to_all(outputs, 'ctx', split_axis=0, concat_axis=0, tiled=True)  6.97 us
    all_to_all x1, starting transfers between devices, local(): lax.all_to_all(send_q, 'ctx', split_axis=0, concat_axis=0, tiled=True)  6.29 us
  transfers between devices with their start and end apart: 3, of which 3 were waited for; matrix products, arithmetic and copies ran while one was open for 4% of the time, Pallas kernels for 0%

commit v1 on v0

v1 whole, which is shorter than its diff:
```python
import functools

import jax
import jax.numpy as jnp
from jax import lax
from jax.experimental import pallas as pl
from jax.experimental.pallas import tpu as pltpu
from jax.sharding import PartitionSpec as P

CAP = 2
MESH = pl.DeviceIdType.MESH
NT = (((1,), (1,)), ((), ()))


def softmax_block(query, key, value, scale, mask):
    scores = lax.dot_general(query, key, NT, preferred_element_type=jnp.float32) * scale
    if mask is not None:
        scores = jnp.where(mask, scores, jnp.float32(-1e30))
    top = jnp.max(scores, axis=-1, keepdims=True)
    prob = jnp.exp(scores - top)
    total = jnp.sum(prob, axis=-1, keepdims=True)
    part = jnp.dot(prob.astype(jnp.bfloat16), value, preferred_element_type=jnp.float32)
    return part * (1.0 / total), top + jnp.log(total)


def kernel(
    dims,
    tbl,
    q_hbm,
    k_hbm,
    v_hbm,
    w_hbm,
    out_ref,
    q,
    k,
    v,
    w,
    qsend,
    osend,
    ssend,
    own,
    own_lse,
    att,
    acc,
    load_sem,
    qs_sem,
    qr_sem,
    os_sem,
    or_sem,
    ss_sem,
    sr_sem,
    as_sem,
    ar_sem,
    *grouped,
):
    n, nh, heads, tiles, rows, width, groups = dims
    per = heads // groups
    tokens = tiles * rows
    scale = width ** (-0.5)
    qrecv, orecv, srecv, lse_cols = (
        grouped[i * groups : (i + 1) * groups] for i in range(4)
    )
    me = lax.axis_index("ctx")
    hd = lax.axis_index("head")
    pick_at = n * heads * CAP
    slot_at = pick_at + heads * tiles * 2

    loads = [
        pltpu.make_async_copy(src, dst, load_sem.at[i])
        for i, (src, dst) in enumerate(((q_hbm, q), (k_hbm, k), (v_hbm, v), (w_hbm, w)))
    ]
    for copy in loads:
        copy.start()

    barrier = pltpu.get_barrier_semaphore()

    def greet(d, _):
        pl.semaphore_signal(
            barrier, inc=1, device_id={"ctx": lax.rem(me + d, n)}, device_id_type=MESH
        )
        return 0

    lax.fori_loop(1, n, greet, 0)
    for j in range(1, nh):
        pl.semaphore_signal(
            barrier, inc=1, device_id={"head": lax.rem(hd + j, nh)}, device_id_type=MESH
        )

    def distance(i):
        half = (i + 1) // 2
        return n // 2 + jnp.where(i % 2 == 0, half, -half)

    def q_copy(g, there, here):
        return pltpu.make_async_remote_copy(
            src_ref=qsend.at[g, there],
            dst_ref=qrecv[g].at[here],
            send_sem=qs_sem.at[g, there],
            recv_sem=qr_sem.at[g, here],
            device_id={"ctx": there},
            device_id_type=MESH,
        )

    def o_copy(g, there, here):
        return pltpu.make_async_remote_copy(
            src_ref=osend.at[g, there],
            dst_ref=orecv[g].at[here],
            send_sem=os_sem.at[g, there],
            recv_sem=or_sem.at[g, here],
            device_id={"ctx": there},
            device_id_type=MESH,
        )

    def s_copy(g, there, here):
        return pltpu.make_async_remote_copy(
            src_ref=ssend.at[g, there],
            dst_ref=srecv[g].at[here],
            send_sem=ss_sem.at[g, there],
            recv_sem=sr_sem.at[g, here],
            device_id={"ctx": there},
            device_id_type=MESH,
        )

    def a_copy(g, there, here):
        return pltpu.make_async_remote_copy(
            src_ref=att.at[here, g],
            dst_ref=att.at[here, g],
            send_sem=as_sem.at[there, g],
            recv_sem=ar_sem.at[here, g],
            device_id={"head": there},
            device_id_type=MESH,
        )

    loads[0].wait()
    pl.semaphore_wait(barrier, n - 1 + nh - 1)

    for g in range(groups):

        def send_queries(i, _, g=g):
            there = me - distance(i)

            @pl.when(there >= 0)
            def _():
                for hh in range(per):
                    h = g * per + hh
                    for s in range(CAP):
                        tile = tbl[(there * heads + h) * CAP + s]
                        qsend[g, there, hh, s] = q[tile, :, h * width : (h + 1) * width]
                q_copy(g, there, me).start()

            return 0

        lax.fori_loop(0, n - 1, send_queries, 0)

    loads[1].wait()
    loads[2].wait()
    lane = lax.broadcasted_iota(jnp.int32, (tokens, 128), 1)
    causal = lax.broadcasted_iota(jnp.int32, (tokens, tokens), 0) >= lax.broadcasted_iota(
        jnp.int32, (tokens, tokens), 1
    )
    lses = jnp.zeros((tokens, 128), jnp.float32)
    for h in range(heads):
        cols = slice(h * width, (h + 1) * width)
        query = q[:, :, cols].reshape(tokens, width)
        part, lse = softmax_block(query, k[:, cols], v[:, cols], scale, causal)
        own[h] = part.reshape(tiles, rows, width)
        lses = jnp.where(lane == h, lse, lses)
    own_lse[...] = lses.reshape(tiles, rows, 128)

    short = CAP * rows
    lane_short = lax.broadcasted_iota(jnp.int32, (short, 128), 1)
    for g in range(groups):
        orecv[g][me] = jnp.zeros((per, CAP, rows, width), jnp.bfloat16)

        def answer(i, _, g=g):
            there = me + distance(i)

            @pl.when(there < n)
            def _():
                q_copy(g, me, there).wait_recv()
                stats = jnp.zeros((short, 128), jnp.float32)
                for hh in range(per):
                    h = g * per + hh
                    cols = slice(h * width, (h + 1) * width)
                    query = qrecv[g][there, hh].reshape(short, width)
                    part, lse = softmax_block(query, k[:, cols], v[:, cols], scale, None)
                    osend[g, there, hh] = part.astype(jnp.bfloat16).reshape(CAP, rows, width)
                    stats = jnp.where(lane_short == hh, lse, stats)
                stats = jnp.concatenate([stats, jnp.zeros((128 - short, 128), jnp.float32)], 0)
                ssend[g, there] = jnp.transpose(stats)[:8]
                o_copy(g, there, me).start()
                s_copy(g, there, me).start()

            return 0

        lax.fori_loop(0, n - 1, answer, 0)

    loads[3].wait()
    part_cols = min(256, out_ref.shape[1])

    def project(p, g, first):
        def body(c, _):
            at = pl.ds(pl.multiple_of(c * part_cols, part_cols), part_cols)
            term = jnp.dot(att[p, g], w[p, g, :, at], preferred_element_type=jnp.float32)
            if first:
                acc[:, at] = term
            else:
                acc[:, at] += term
            return 0

        lax.fori_loop(0, out_ref.shape[1] // part_cols, body, 0)

    for g in range(groups):
        lse_cols[g][me] = jnp.full((CAP, rows, 8), -1e30, jnp.float32)

        def collect(i, _, g=g):
            there = me - distance(i)

            @pl.when(there >= 0)
            def _():
                s_copy(g, me, there).wait_recv()
                lse_cols[g][there] = jnp.transpose(srecv[g][there])[:short].reshape(CAP, rows, 8)
                o_copy(g, me, there).wait_recv()

            return 0

        lax.fori_loop(0, n - 1, collect, 0)

        def combine(t, _, g=g):
            for hh in range(per):
                h = g * per + hh
                at = (h * tiles + t) * 2
                a1, a2 = tbl[pick_at + at], tbl[pick_at + at + 1]
                s1, s2 = tbl[slot_at + at], tbl[slot_at + at + 1]
                l0 = own_lse[t, :, h : h + 1]
                l1 = lse_cols[g][a1, s1][:, hh : hh + 1]
                l2 = lse_cols[g][a2, s2][:, hh : hh + 1]
                top = jnp.maximum(l0, jnp.maximum(l1, l2))
                w0, w1, w2 = jnp.exp(l0 - top), jnp.exp(l1 - top), jnp.exp(l2 - top)
                inv = 1.0 / (w0 + w1 + w2)
                o1 = orecv[g][a1, hh, s1].astype(jnp.float32)
                o2 = orecv[g][a2, hh, s2].astype(jnp.float32)
                mixed = (w0 * inv) * own[h, t] + (w1 * inv) * o1 + (w2 * inv) * o2
                att[hd, g, pl.ds(pl.multiple_of(t * rows, rows), rows), hh * width : (hh + 1) * width] = (
                    mixed.astype(jnp.bfloat16)
                )
            return 0

        lax.fori_loop(0, tiles, combine, 0)
        for j in range(1, nh):
            a_copy(g, lax.rem(hd + j, nh), hd).start()

    for g in range(groups):
        project(hd, g, g == 0)
    for g in range(groups):
        for j in range(1, nh):
            peer = lax.rem(hd + j, nh)
            a_copy(g, hd, peer).wait_recv()
            project(peer, g, False)
    out_ref[...] = acc[...].astype(out_ref.dtype)

    for g in range(groups):

        def drain(i, _, g=g):
            d = distance(i)

            @pl.when(me - d >= 0)
            def _():
                q_copy(g, me - d, me).wait_send()

            @pl.when(me + d < n)
            def _():
                o_copy(g, me + d, me).wait_send()
                s_copy(g, me + d, me).wait_send()

            return 0

        lax.fori_loop(0, n - 1, drain, 0)
        for j in range(1, nh):
            a_copy(g, lax.rem(hd + j, nh), hd).wait_send()


def tables(selected, n):
    heads, tiles, _ = selected.shape
    picks = selected[:, :, 1:].reshape(heads, tiles * 2)
    order = jnp.arange(tiles * 2, dtype=jnp.int32)
    same = (picks[:, :, None] == picks[:, None, :]) & (order[None, :] < order[:, None])
    slot = jnp.minimum(jnp.sum(same.astype(jnp.int32), axis=-1), CAP - 1)
    hit = (picks[None, :, None, :] == jnp.arange(n, dtype=jnp.int32)[:, None, None, None]) & (
        slot[None, :, None, :] == jnp.arange(CAP, dtype=jnp.int32)[None, None, :, None]
    )
    tile = jnp.max(jnp.where(hit, order // 2, 0), axis=-1)
    return jnp.concatenate([tile.reshape(-1), picks.reshape(-1), slot.reshape(-1)])


def solution(mesh):
    n, nh = mesh.shape["ctx"], mesh.shape["head"]

    def local(queries, keys, values, selected, out_weight):
        heads, tiles = selected.shape[:2]
        tokens, cols = queries.shape[0], out_weight.shape[1]
        width = queries.shape[1] // heads
        rows = tokens // tiles
        groups = 2 if heads % 2 == 0 and heads >= 4 else 1
        per = heads // groups
        bf16, f32 = jnp.bfloat16, jnp.float32
        dma = pltpu.SemaphoreType.DMA
        packet = (n, per, CAP, rows, width)
        grouped = (
            [pltpu.VMEM(packet, bf16)] * (2 * groups)
            + [pltpu.VMEM((n, 8, 128), f32)] * groups
            + [pltpu.VMEM((n, CAP, rows, 8), f32)] * groups
        )
        weight = out_weight.reshape(nh, groups, per * width, cols)
        return pl.pallas_call(
            functools.partial(kernel, (n, nh, heads, tiles, rows, width, groups)),
            out_shape=jax.ShapeDtypeStruct((tokens, cols), bf16),
            in_specs=[pl.BlockSpec(memory_space=pltpu.SMEM)]
            + [pl.BlockSpec(memory_space=pl.ANY)] * 4,
            out_specs=pl.BlockSpec(memory_space=pltpu.VMEM),
            scratch_shapes=[
                pltpu.VMEM((tiles, rows, heads * width), bf16),
                pltpu.VMEM((tokens, heads * width), bf16),
                pltpu.VMEM((tokens, heads * width), bf16),
                pltpu.VMEM(weight.shape, bf16),
                pltpu.VMEM((groups,) + packet, bf16),
                pltpu.VMEM((groups,) + packet, bf16),
                pltpu.VMEM((groups, n, 8, 128), f32),
                pltpu.VMEM((heads, tiles, rows, width), f32),
                pltpu.VMEM((tiles, rows, 128), f32),
                pltpu.VMEM((nh, groups, tokens, per * width), bf16),
                pltpu.VMEM((tokens, cols), f32),
                dma((4,)),
                dma((groups, n)),
                dma((groups, n)),
                dma((groups, n)),
                dma((groups, n)),
                dma((groups, n)),
                dma((groups, n)),
                dma((nh, groups)),
                dma((nh, groups)),
            ]
            + grouped,
            compiler_params=pltpu.CompilerParams(
                collective_id=0, has_side_effects=True, vmem_limit_bytes=56 * 1024 * 1024
            ),
        )(
            tables(selected, n),
            queries.reshape(tiles, rows, heads * width),
            keys,
            values,
            weight,
        )

    return jax.shard_map(
        local,
        mesh=mesh,
        in_specs=(
            P("ctx", "head"),
            P("ctx", "head"),
            P("ctx", "head"),
            P("head", "ctx", None),
            P(None, "head"),
        ),
        out_specs=P("ctx", "head"),
        check_vma=False,
    )
```

time: 276 us -> 89.7 us (0.33); the launches traced: 272 us -> 89.5 us
  waiting for transfers between devices: 150 us -> 0 us
  Pallas kernels: 0 us -> 84.5 us
  matrix products: 46.3 us -> 0 us
  local copies, waits for them, and re-layouts: 30.7 us -> 3.37 us
  between operations: 13.6 us -> 0.04 us
  starting transfers between devices: 13.3 us -> 0 us
  blocking collectives: 8.67 us -> 0 us
  other arithmetic: 9.04 us -> 1.55 us
    all_to_all x2 -> x0, waiting for transfers between devices: 129 us -> none  [the longest x1 85.8 us: partials_back(): lax.all_to_all(outputs, 'ctx', split_axis=0, concat_axis=0, tiled=True)]
    pallas_call x0 -> x1, Pallas kernels: none -> 84.5 us  [local(): pl.pallas_call(functools.partial(kernel, (n, nh, heads, tiles, rows, widt...]
    dot_general x35 -> x0, matrix products: 46.3 us -> none  [the longest x16 32.9 us: owner_block(): jnp.einsum('gchtk,khd->gchtd', prob.astype(jnp.bfloat16), vals_three, pre...]
    all_gather x1 -> x0, waiting for transfers between devices: 21.1 us -> none  [local(): lax.all_gather(attention, 'head', axis=1, tiled=True)]
    scatter x1 -> x0, local copies, waits for them, and re-layouts: 14.8 us -> none  [local(): send_q = send_q.at[target, slot, head_idx].set(query_pairs, mode='drop')]
    all_to_all x2 -> x0, starting transfers between devices: 13.3 us -> none  [the longest x1 6.97 us: partials_back(): lax.all_to_all(outputs, 'ctx', split_axis=0, concat_axis=0, tiled=True)]
    all_to_all x1 -> x0, blocking collectives: 8.67 us -> none  [partials_back(): lax.all_to_all(sums, 'ctx', split_axis=0, concat_axis=0, tiled=True)]
    reduce_sum x19 -> x1, other arithmetic: 6.06 us -> 0.29 us  [tables(): slot = jnp.minimum(jnp.sum(same.astype(jnp.int32), axis=-1), CAP - 1)]
  transfers between devices with their start and end apart: 3 -> 0, of which waited for: 3 -> 0; matrix products, arithmetic and copies ran while one was open for 4% -> 0% of each run, Pallas kernels for 0% -> 0%
where the time goes in v1:
time: 89.7 us; the launch traced here: 89.5 us
  Pallas kernels  84.5 us (94%)
  local copies, waits for them, and re-layouts  3.37 us (4%)
  other arithmetic  1.55 us (2%)
    pallas_call x1, Pallas kernels, local(): pl.pallas_call(functools.partial(kernel, (n, nh, heads, tiles, rows, widt...  84.5 us
    unnamed x1, local copies, waits for them, and re-layouts  1.87 us

profile of v1, /device:TPU:16, one launch (start us, length us, event | category | flops | bytes accessed | tf_op | source)
XLA Modules:
  0.0 89.5 jit_solution(10908846187000090823)
XLA Ops:
  0.0 0.7 slice.3
  0.7 0.1 copy.16
  0.8 0.1 copy.17
  0.9 0.3 convert_reduce_fusion
  1.2 0.1 min.16
  1.3 0.6 select_reduce_fusion
  1.9 0.1 copy.21
  2.0 0.1 reshape_reshape.3
  2.2 0.2 copy.20
  2.4 0.1 reshape.45
  2.5 0.6 pad_add_fusion.tbl
  3.1 84.5 %shard_map.55 = bf16[256,1024]{1,0:T(8,128)(2,1)} custom-call(s32[512]{0:T(512)} %pad_add_fusion.tbl, bf16[8,32,1024]{2,1,0:T(8,128)(2,1)} %bitcast.4, bf16[256,1024]{1,0:T(8,128)(2,1)} %k_hbm.1, bf16[256,1024]{1,0:T(8,128)(2,1)} %v_hbm.1, bf16[2,2,512,1024]{3,2,1,0:T(8,128)(2,1)} %bitcast.3), custom_call_target="tpu_custom_call" | custom-call | tf_op jit(solution)/shard_map/pallas_call | solution.py:314
  87.6 1.9 %copy.23 = bf16[256,1024]{1,0:T(8,128)(2,1)} copy(bf16[256,1024]{1,0:T(8,128)(2,1)} %shard_map.55) | data formatting | bytes 1048576
  (5 shorter events, 0.0 us)

commit v2 on v1

--- a/solution.py
+++ b/solution.py
@@ -8,24 +8,56 @@
 from jax.sharding import PartitionSpec as P
 
 CAP = 2
+AHEAD = 2
+LAG = 2
 MESH = pl.DeviceIdType.MESH
+LOG2E = 1.4426950408889634
 NT = (((1,), (1,)), ((), ()))
 
 
 def softmax_block(query, key, value, scale, mask):
-    scores = lax.dot_general(query, key, NT, preferred_element_type=jnp.float32) * scale
+    scores = lax.dot_general(query, key, NT, preferred_element_type=jnp.float32)
     if mask is not None:
         scores = jnp.where(mask, scores, jnp.float32(-1e30))
     top = jnp.max(scores, axis=-1, keepdims=True)
-    prob = jnp.exp(scores - top)
+    prob = jnp.exp2((scores - top) * (scale * LOG2E))
     total = jnp.sum(prob, axis=-1, keepdims=True)
     part = jnp.dot(prob.astype(jnp.bfloat16), value, preferred_element_type=jnp.float32)
-    return part * (1.0 / total), top + jnp.log(total)
+    return part * (1.0 / total), top * scale + jnp.log(total)
+
+
+def fill_tables(n, tiles, sel, tblv):
+    heads, entries = sel.shape
+    each = entries // tiles
+    picks = sel[...]
+    lane = lax.broadcasted_iota(jnp.int32, (heads, entries), 1)
+    tile_of = jnp.zeros((heads, entries), jnp.int32)
+    for t in range(1, tiles):
+        tile_of += jnp.where(lane >= t * each, 1, 0)
+    other = lane != tile_of * each
+    rank = jnp.zeros((heads, entries), jnp.int32)
+    for j in range(entries):
+        if j % each != 0:
+            rank += jnp.where((picks == picks[:, j : j + 1]) & (lane > j) & other, 1, 0)
+    slot = jnp.minimum(rank, CAP - 1)
+    lanes = tblv.shape[2]
+    wide = lax.broadcasted_iota(jnp.int32, (heads, lanes), 1)
+    found = jnp.zeros((heads, lanes), jnp.int32)
+    for a in range(n):
+        for s in range(CAP):
+            hit = other & (picks == a) & (slot == s)
+            tile = jnp.max(jnp.where(hit, tile_of, 0), axis=1, keepdims=True)
+            found = jnp.where(wide == a * CAP + s, tile, found)
+    tblv[0] = found
+    tblv[1] = jnp.zeros((heads, lanes), jnp.int32)
+    tblv[2] = jnp.zeros((heads, lanes), jnp.int32)
+    tblv[1, :, :entries] = picks
+    tblv[2, :, :entries] = slot
 
 
 def kernel(
     dims,
-    tbl,
+    sel,
     q_hbm,
     k_hbm,
     v_hbm,
@@ -42,6 +74,8 @@
     own_lse,
     att,
     acc,
+    tblv,
+    tbl,
     load_sem,
     qs_sem,
     qr_sem,
@@ -57,13 +91,9 @@
     per = heads // groups
     tokens = tiles * rows
     scale = width ** (-0.5)
-    qrecv, orecv, srecv, lse_cols = (
-        grouped[i * groups : (i + 1) * groups] for i in range(4)
-    )
+    qrecv, orecv, srecv = (grouped[i * groups : (i + 1) * groups] for i in range(3))
     me = lax.axis_index("ctx")
     hd = lax.axis_index("head")
-    pick_at = n * heads * CAP
-    slot_at = pick_at + heads * tiles * 2
 
     loads = [
         pltpu.make_async_copy(src, dst, load_sem.at[i])
@@ -130,12 +160,15 @@
             device_id_type=MESH,
         )
 
+    fill_tables(n, tiles, sel, tblv)
+    to_scalars = pltpu.make_async_copy(tblv, tbl, load_sem.at[4])
+    to_scalars.start()
     loads[0].wait()
+    to_scalars.wait()
     pl.semaphore_wait(barrier, n - 1 + nh - 1)
 
-    for g in range(groups):
-
-        def send_queries(i, _, g=g):
+    def send_group(g):
+        def send_queries(i, _):
             there = me - distance(i)
 
             @pl.when(there >= 0)
@@ -143,7 +176,7 @@
                 for hh in range(per):
                     h = g * per + hh
                     for s in range(CAP):
-                        tile = tbl[(there * heads + h) * CAP + s]
+                        tile = tbl[0, h, there * CAP + s]
                         qsend[g, there, hh, s] = q[tile, :, h * width : (h + 1) * width]
                 q_copy(g, there, me).start()
 
@@ -151,42 +184,44 @@
 
         lax.fori_loop(0, n - 1, send_queries, 0)
 
+    for g in range(min(AHEAD, groups)):
+        send_group(g)
     loads[1].wait()
     loads[2].wait()
-    lane = lax.broadcasted_iota(jnp.int32, (tokens, 128), 1)
     causal = lax.broadcasted_iota(jnp.int32, (tokens, tokens), 0) >= lax.broadcasted_iota(
         jnp.int32, (tokens, tokens), 1
     )
-    lses = jnp.zeros((tokens, 128), jnp.float32)
     for h in range(heads):
         cols = slice(h * width, (h + 1) * width)
         query = q[:, :, cols].reshape(tokens, width)
         part, lse = softmax_block(query, k[:, cols], v[:, cols], scale, causal)
         own[h] = part.reshape(tiles, rows, width)
-        lses = jnp.where(lane == h, lse, lses)
-    own_lse[...] = lses.reshape(tiles, rows, 128)
+        own_lse[h] = jnp.broadcast_to(lse, (tokens, width)).reshape(tiles, rows, width)
 
     short = CAP * rows
-    lane_short = lax.broadcasted_iota(jnp.int32, (short, 128), 1)
-    for g in range(groups):
+    stat_lanes = ssend.shape[3]
+    lane = lax.broadcasted_iota(jnp.int32, (short, stat_lanes), 1)
+    row = lax.broadcasted_iota(jnp.int32, (short, stat_lanes), 0)
+
+    def answer_group(g):
         orecv[g][me] = jnp.zeros((per, CAP, rows, width), jnp.bfloat16)
-
-        def answer(i, _, g=g):
+        srecv[g][me] = jnp.full((1, stat_lanes), -1e30, jnp.float32)
+
+        def answer(i, _):
             there = me + distance(i)
 
             @pl.when(there < n)
             def _():
                 q_copy(g, me, there).wait_recv()
-                stats = jnp.zeros((short, 128), jnp.float32)
+                stats = jnp.zeros((short, stat_lanes), jnp.float32)
                 for hh in range(per):
                     h = g * per + hh
                     cols = slice(h * width, (h + 1) * width)
                     query = qrecv[g][there, hh].reshape(short, width)
                     part, lse = softmax_block(query, k[:, cols], v[:, cols], scale, None)
                     osend[g, there, hh] = part.astype(jnp.bfloat16).reshape(CAP, rows, width)
-                    stats = jnp.where(lane_short == hh, lse, stats)
-                stats = jnp.concatenate([stats, jnp.zeros((128 - short, 128), jnp.float32)], 0)
-                ssend[g, there] = jnp.transpose(stats)[:8]
+                    stats = jnp.where(lane == row + hh * short, lse, stats)
+                ssend[g, there] = jnp.sum(stats, axis=0, keepdims=True)
                 o_copy(g, there, me).start()
                 s_copy(g, there, me).start()
 
@@ -194,7 +229,6 @@
 
         lax.fori_loop(0, n - 1, answer, 0)
 
-    loads[3].wait()
     part_cols = min(256, out_ref.shape[1])
 
     def project(p, g, first):
@@ -209,46 +243,55 @@
 
         lax.fori_loop(0, out_ref.shape[1] // part_cols, body, 0)
 
-    for g in range(groups):
-        lse_cols[g][me] = jnp.full((CAP, rows, 8), -1e30, jnp.float32)
-
-        def collect(i, _, g=g):
+    lane_tile = lax.broadcasted_iota(jnp.int32, (rows, stat_lanes), 1)
+    lane_tile = lane_tile - lax.broadcasted_iota(jnp.int32, (rows, stat_lanes), 0)
+
+    def collect_group(g):
+        def collect(i, _):
             there = me - distance(i)
 
             @pl.when(there >= 0)
             def _():
                 s_copy(g, me, there).wait_recv()
-                lse_cols[g][there] = jnp.transpose(srecv[g][there])[:short].reshape(CAP, rows, 8)
                 o_copy(g, me, there).wait_recv()
 
             return 0
 
         lax.fori_loop(0, n - 1, collect, 0)
 
-        def combine(t, _, g=g):
+        def picked_lse(block, slot, hh):
+            hit = lane_tile == hh * short + slot * rows
+            return jnp.sum(jnp.where(hit, srecv[g][block], 0.0), axis=1, keepdims=True)
+
+        def combine(t, _):
             for hh in range(per):
                 h = g * per + hh
-                at = (h * tiles + t) * 2
-                a1, a2 = tbl[pick_at + at], tbl[pick_at + at + 1]
-                s1, s2 = tbl[slot_at + at], tbl[slot_at + at + 1]
-                l0 = own_lse[t, :, h : h + 1]
-                l1 = lse_cols[g][a1, s1][:, hh : hh + 1]
-                l2 = lse_cols[g][a2, s2][:, hh : hh + 1]
+                a1, a2 = tbl[1, h, t * 3 + 1], tbl[1, h, t * 3 + 2]
+                s1, s2 = tbl[2, h, t * 3 + 1], tbl[2, h, t * 3 + 2]
+                l0 = own_lse[h, t]
+                l1, l2 = picked_lse(a1, s1, hh), picked_lse(a2, s2, hh)
                 top = jnp.maximum(l0, jnp.maximum(l1, l2))
                 w0, w1, w2 = jnp.exp(l0 - top), jnp.exp(l1 - top), jnp.exp(l2 - top)
-                inv = 1.0 / (w0 + w1 + w2)
                 o1 = orecv[g][a1, hh, s1].astype(jnp.float32)
                 o2 = orecv[g][a2, hh, s2].astype(jnp.float32)
-                mixed = (w0 * inv) * own[h, t] + (w1 * inv) * o1 + (w2 * inv) * o2
-                att[hd, g, pl.ds(pl.multiple_of(t * rows, rows), rows), hh * width : (hh + 1) * width] = (
-                    mixed.astype(jnp.bfloat16)
-                )
+                mixed = (w0 * own[h, t] + w1 * o1 + w2 * o2) / (w0 + w1 + w2)
+                at = pl.ds(pl.multiple_of(t * rows, rows), rows)
+                att[hd, g, at, hh * width : (hh + 1) * width] = mixed.astype(jnp.bfloat16)
             return 0
 
         lax.fori_loop(0, tiles, combine, 0)
         for j in range(1, nh):
             a_copy(g, lax.rem(hd + j, nh), hd).start()
 
+    for g in range(groups):
+        answer_group(g)
+        if g + AHEAD < groups:
+            send_group(g + AHEAD)
+        if g >= LAG:
+            collect_group(g - LAG)
+    for g in range(max(groups - LAG, 0), groups):
+        collect_group(g)
+    loads[3].wait()
     for g in range(groups):
         project(hd, g, g == 0)
     for g in range(groups):
@@ -279,19 +322,6 @@
             a_copy(g, lax.rem(hd + j, nh), hd).wait_send()
 
 
-def tables(selected, n):
-    heads, tiles, _ = selected.shape
-    picks = selected[:, :, 1:].reshape(heads, tiles * 2)
-    order = jnp.arange(tiles * 2, dtype=jnp.int32)
-    same = (picks[:, :, None] == picks[:, None, :]) & (order[None, :] < order[:, None])
-    slot = jnp.minimum(jnp.sum(same.astype(jnp.int32), axis=-1), CAP - 1)
-    hit = (picks[None, :, None, :] == jnp.arange(n, dtype=jnp.int32)[:, None, None, None]) & (
-        slot[None, :, None, :] == jnp.arange(CAP, dtype=jnp.int32)[None, None, :, None]
-    )
-    tile = jnp.max(jnp.where(hit, order // 2, 0), axis=-1)
-    return jnp.concatenate([tile.reshape(-1), picks.reshape(-1), slot.reshape(-1)])
-
-
 def solution(mesh):
     n, nh = mesh.shape["ctx"], mesh.shape["head"]
 
@@ -300,21 +330,22 @@
         tokens, cols = queries.shape[0], out_weight.shape[1]
         width = queries.shape[1] // heads
         rows = tokens // tiles
-        groups = 2 if heads % 2 == 0 and heads >= 4 else 1
-        per = heads // groups
+        per = 2 if heads % 2 == 0 and heads >= 4 else 1
+        groups = heads // per
+        stat_lanes = -(-per * CAP * rows // 128) * 128
+        table = (3, heads, -(-max(n * CAP, tiles * 3) // 128) * 128)
         bf16, f32 = jnp.bfloat16, jnp.float32
         dma = pltpu.SemaphoreType.DMA
         packet = (n, per, CAP, rows, width)
         grouped = (
             [pltpu.VMEM(packet, bf16)] * (2 * groups)
-            + [pltpu.VMEM((n, 8, 128), f32)] * groups
-            + [pltpu.VMEM((n, CAP, rows, 8), f32)] * groups
+            + [pltpu.VMEM((n, 1, stat_lanes), f32)] * groups
         )
         weight = out_weight.reshape(nh, groups, per * width, cols)
         return pl.pallas_call(
             functools.partial(kernel, (n, nh, heads, tiles, rows, width, groups)),
             out_shape=jax.ShapeDtypeStruct((tokens, cols), bf16),
-            in_specs=[pl.BlockSpec(memory_space=pltpu.SMEM)]
+            in_specs=[pl.BlockSpec(memory_space=pltpu.VMEM)]
             + [pl.BlockSpec(memory_space=pl.ANY)] * 4,
             out_specs=pl.BlockSpec(memory_space=pltpu.VMEM),
             scratch_shapes=[
@@ -324,12 +355,14 @@
                 pltpu.VMEM(weight.shape, bf16),
                 pltpu.VMEM((groups,) + packet, bf16),
                 pltpu.VMEM((groups,) + packet, bf16),
-                pltpu.VMEM((groups, n, 8, 128), f32),
+                pltpu.VMEM((groups, n, 1, stat_lanes), f32),
                 pltpu.VMEM((heads, tiles, rows, width), f32),
-                pltpu.VMEM((tiles, rows, 128), f32),
+                pltpu.VMEM((heads, tiles, rows, width), f32),
                 pltpu.VMEM((nh, groups, tokens, per * width), bf16),
                 pltpu.VMEM((tokens, cols), f32),
-                dma((4,)),
+                pltpu.VMEM(table, jnp.int32),
+                pltpu.SMEM(table, jnp.int32),
+                dma((5,)),
                 dma((groups, n)),
                 dma((groups, n)),
                 dma((groups, n)),
@@ -344,7 +377,7 @@
                 collective_id=0, has_side_effects=True, vmem_limit_bytes=56 * 1024 * 1024
             ),
         )(
-            tables(selected, n),
+            selected.reshape(heads, -1),
             queries.reshape(tiles, rows, heads * width),
             keys,
             values,

time: 89.7 us -> 83.8 us (0.934)
  Pallas kernels: 84.5 us -> 79.6 us
  other arithmetic: 1.55 us -> 0 us
    pallas_call x1, Pallas kernels: 84.5 us -> 79.6 us  [local(): pl.pallas_call(functools.partial(kernel, (n, nh, heads, tiles, rows, widt...]
    slice x3 -> x0, local copies, waits for them, and re-layouts: 0.9 us -> none  [tables(): picks = selected[:, :, 1:].reshape(heads, tiles * 2)]
    unnamed x1 -> x2, local copies, waits for them, and re-layouts: 1.87 us -> 2.65 us
where the time goes in v2:
time: 83.8 us; the launch traced here: 82.9 us
  Pallas kernels  79.6 us (95%)
  local copies, waits for them, and re-layouts  3.33 us (4%)
    pallas_call x1, Pallas kernels, local(): pl.pallas_call(functools.partial(kernel, (n, nh, heads, tiles, rows, widt...  79.6 us
    unnamed x2, local copies, waits for them, and re-layouts  2.65 us

profile of v2, /device:TPU:16, one launch (start us, length us, event | category | flops | bytes accessed | tf_op | source)
XLA Modules:
  0.0 82.9 jit_solution(8079771537498380442)
XLA Ops:
  0.0 0.8 copy.7
  0.8 0.7 copy.8.sel
  1.5 79.6 %shard_map.55 = bf16[256,1024]{1,0:T(8,128)(2,1)} custom-call(s32[8,24]{1,0:T(8,128)} %copy.8.sel, bf16[8,32,1024]{2,1,0:T(8,128)(2,1)} %bitcast.5, bf16[256,1024]{1,0:T(8,128)(2,1)} %k_hbm.1, bf16[256,1024]{1,0:T(8,128)(2,1)} %v_hbm.1, bf16[2,4,256,1024]{3,2,1,0:T(8,128)(2,1)} %bitcast.4), custom_call_target="tpu_custom_call" | custom-call | tf_op jit(solution)/shard_map/pallas_call | solution.py:345
  81.1 1.9 %copy.10 = bf16[256,1024]{1,0:T(8,128)(2,1)} copy(bf16[256,1024]{1,0:T(8,128)(2,1)} %shard_map.55) | data formatting | bytes 1048576
  (1 shorter events, 0.0 us)

commit v3 on v2

--- a/solution.py
+++ b/solution.py
@@ -10,6 +10,7 @@
 CAP = 2
 AHEAD = 2
 LAG = 2
+TEAM = 4
 MESH = pl.DeviceIdType.MESH
 LOG2E = 1.4426950408889634
 NT = (((1,), (1,)), ((), ()))
@@ -27,10 +28,16 @@
 
 
 def fill_tables(n, tiles, sel, tblv):
-    heads, entries = sel.shape
-    each = entries // tiles
-    picks = sel[...]
+    heads, _, each = sel.shape
+    entries = tiles * each
     lane = lax.broadcasted_iota(jnp.int32, (heads, entries), 1)
+    picks = jnp.zeros((heads, entries), jnp.int32)
+    column = []
+    for t in range(tiles):
+        chosen = sel[:, t, :]
+        for r in range(each):
+            column.append(chosen[:, r : r + 1])
+            picks = jnp.where(lane == t * each + r, column[-1], picks)
     tile_of = jnp.zeros((heads, entries), jnp.int32)
     for t in range(1, tiles):
         tile_of += jnp.where(lane >= t * each, 1, 0)
@@ -38,7 +45,7 @@
     rank = jnp.zeros((heads, entries), jnp.int32)
     for j in range(entries):
         if j % each != 0:
-            rank += jnp.where((picks == picks[:, j : j + 1]) & (lane > j) & other, 1, 0)
+            rank += jnp.where((picks == column[j]) & (lane > j) & other, 1, 0)
     slot = jnp.minimum(rank, CAP - 1)
     lanes = tblv.shape[2]
     wide = lax.broadcasted_iota(jnp.int32, (heads, lanes), 1)
@@ -116,9 +123,15 @@
             barrier, inc=1, device_id={"head": lax.rem(hd + j, nh)}, device_id_type=MESH
         )
 
+    level, place = me // TEAM, lax.rem(me, TEAM)
+    levels = n // TEAM
+
     def distance(i):
         half = (i + 1) // 2
-        return n // 2 + jnp.where(i % 2 == 0, half, -half)
+        return levels // 2 + jnp.where(i % 2 == 0, half, -half)
+
+    def member(at_level, j):
+        return at_level * TEAM + lax.rem(place + j, TEAM)
 
     def q_copy(g, there, here):
         return pltpu.make_async_remote_copy(
@@ -169,9 +182,9 @@
 
     def send_group(g):
         def send_queries(i, _):
-            there = me - distance(i)
-
-            @pl.when(there >= 0)
+            there = member(level - distance(i // TEAM), lax.rem(i, TEAM))
+
+            @pl.when((there >= 0) & (there < me))
             def _():
                 for hh in range(per):
                     h = g * per + hh
@@ -182,7 +195,7 @@
 
             return 0
 
-        lax.fori_loop(0, n - 1, send_queries, 0)
+        lax.fori_loop(0, n, send_queries, 0)
 
     for g in range(min(AHEAD, groups)):
         send_group(g)
@@ -200,45 +213,61 @@
 
     short = CAP * rows
     stat_lanes = ssend.shape[3]
-    lane = lax.broadcasted_iota(jnp.int32, (short, stat_lanes), 1)
-    row = lax.broadcasted_iota(jnp.int32, (short, stat_lanes), 0)
+    lane = lax.broadcasted_iota(jnp.int32, (TEAM, short, stat_lanes), 2)
+    lane = lane - lax.broadcasted_iota(jnp.int32, (TEAM, short, stat_lanes), 1)
 
     def answer_group(g):
         orecv[g][me] = jnp.zeros((per, CAP, rows, width), jnp.bfloat16)
         srecv[g][me] = jnp.full((1, stat_lanes), -1e30, jnp.float32)
 
         def answer(i, _):
-            there = me + distance(i)
-
-            @pl.when(there < n)
+            their = level + distance(i)
+
+            @pl.when(their < levels)
             def _():
-                q_copy(g, me, there).wait_recv()
-                stats = jnp.zeros((short, stat_lanes), jnp.float32)
+                for j in range(TEAM):
+                    there = member(their, j)
+
+                    @pl.when(there > me)
+                    def _():
+                        q_copy(g, me, there).wait_recv()
+
+                team = pl.ds(pl.multiple_of(their * TEAM, TEAM), TEAM)
+                stats = jnp.zeros((TEAM, short, stat_lanes), jnp.float32)
                 for hh in range(per):
                     h = g * per + hh
                     cols = slice(h * width, (h + 1) * width)
-                    query = qrecv[g][there, hh].reshape(short, width)
+                    query = qrecv[g][team, hh].reshape(TEAM * short, width)
                     part, lse = softmax_block(query, k[:, cols], v[:, cols], scale, None)
-                    osend[g, there, hh] = part.astype(jnp.bfloat16).reshape(CAP, rows, width)
-                    stats = jnp.where(lane == row + hh * short, lse, stats)
-                ssend[g, there] = jnp.sum(stats, axis=0, keepdims=True)
-                o_copy(g, there, me).start()
-                s_copy(g, there, me).start()
+                    osend[g, team, hh] = part.astype(jnp.bfloat16).reshape(TEAM, CAP, rows, width)
+                    lse = jnp.broadcast_to(lse, (TEAM * short, stat_lanes))
+                    lse = lse.reshape(TEAM, short, stat_lanes)
+                    stats = jnp.where(lane == hh * short, lse, stats)
+                ssend[g, team] = jnp.sum(stats, axis=1, keepdims=True)
+                for j in range(TEAM):
+                    there = member(their, j)
+
+                    @pl.when(there > me)
+                    def _():
+                        o_copy(g, there, me).start()
+                        s_copy(g, there, me).start()
 
             return 0
 
-        lax.fori_loop(0, n - 1, answer, 0)
+        lax.fori_loop(0, levels, answer, 0)
 
     part_cols = min(256, out_ref.shape[1])
 
-    def project(p, g, first):
+    def project(p, last):
         def body(c, _):
             at = pl.ds(pl.multiple_of(c * part_cols, part_cols), part_cols)
-            term = jnp.dot(att[p, g], w[p, g, :, at], preferred_element_type=jnp.float32)
-            if first:
+            term = 0.0 if p is hd else acc[:, at]
+            for g in range(groups):
+                term += jnp.dot(att[p, g], w[p, g, :, at], preferred_element_type=jnp.float32)
+            if last:
+                out_ref[:, at] = term.astype(out_ref.dtype)
+            else:
                 acc[:, at] = term
-            else:
-                acc[:, at] += term
             return 0
 
         lax.fori_loop(0, out_ref.shape[1] // part_cols, body, 0)
@@ -248,38 +277,38 @@
 
     def collect_group(g):
         def collect(i, _):
-            there = me - distance(i)
-
-            @pl.when(there >= 0)
+            there = member(level - distance(i // TEAM), lax.rem(i, TEAM))
+
+            @pl.when((there >= 0) & (there < me))
             def _():
                 s_copy(g, me, there).wait_recv()
                 o_copy(g, me, there).wait_recv()
 
             return 0
 
-        lax.fori_loop(0, n - 1, collect, 0)
+        lax.fori_loop(0, n, collect, 0)
 
         def picked_lse(block, slot, hh):
             hit = lane_tile == hh * short + slot * rows
             return jnp.sum(jnp.where(hit, srecv[g][block], 0.0), axis=1, keepdims=True)
 
-        def combine(t, _):
-            for hh in range(per):
-                h = g * per + hh
-                a1, a2 = tbl[1, h, t * 3 + 1], tbl[1, h, t * 3 + 2]
-                s1, s2 = tbl[2, h, t * 3 + 1], tbl[2, h, t * 3 + 2]
-                l0 = own_lse[h, t]
-                l1, l2 = picked_lse(a1, s1, hh), picked_lse(a2, s2, hh)
-                top = jnp.maximum(l0, jnp.maximum(l1, l2))
-                w0, w1, w2 = jnp.exp(l0 - top), jnp.exp(l1 - top), jnp.exp(l2 - top)
-                o1 = orecv[g][a1, hh, s1].astype(jnp.float32)
-                o2 = orecv[g][a2, hh, s2].astype(jnp.float32)
-                mixed = (w0 * own[h, t] + w1 * o1 + w2 * o2) / (w0 + w1 + w2)
-                at = pl.ds(pl.multiple_of(t * rows, rows), rows)
-                att[hd, g, at, hh * width : (hh + 1) * width] = mixed.astype(jnp.bfloat16)
-            return 0
-
-        lax.fori_loop(0, tiles, combine, 0)
+        for hh in range(per):
+            h = g * per + hh
+
+            def gather(r):
+                blocks = [tbl[1, h, t * 3 + r] for t in range(tiles)]
+                slots = [tbl[2, h, t * 3 + r] for t in range(tiles)]
+                outs = [orecv[g][a, hh, s] for a, s in zip(blocks, slots)]
+                lses = [picked_lse(a, s, hh) for a, s in zip(blocks, slots)]
+                return jnp.concatenate(outs, 0).astype(jnp.float32), jnp.concatenate(lses, 0)
+
+            (o1, l1), (o2, l2) = gather(1), gather(2)
+            l0 = own_lse[h].reshape(tokens, width)
+            top = jnp.maximum(l0, jnp.maximum(l1, l2))
+            w0, w1, w2 = jnp.exp(l0 - top), jnp.exp(l1 - top), jnp.exp(l2 - top)
+            mixed = w0 * own[h].reshape(tokens, width) + w1 * o1 + w2 * o2
+            mixed = mixed / (w0 + w1 + w2)
+            att[hd, g, :, hh * width : (hh + 1) * width] = mixed.astype(jnp.bfloat16)
         for j in range(1, nh):
             a_copy(g, lax.rem(hd + j, nh), hd).start()
 
@@ -292,20 +321,16 @@
     for g in range(max(groups - LAG, 0), groups):
         collect_group(g)
     loads[3].wait()
+    project(hd, nh == 1)
+    for j in range(1, nh):
+        peer = lax.rem(hd + j, nh)
+        for g in range(groups):
+            a_copy(g, hd, peer).wait_recv()
+        project(peer, j == nh - 1)
+
     for g in range(groups):
-        project(hd, g, g == 0)
-    for g in range(groups):
-        for j in range(1, nh):
-            peer = lax.rem(hd + j, nh)
-            a_copy(g, hd, peer).wait_recv()
-            project(peer, g, False)
-    out_ref[...] = acc[...].astype(out_ref.dtype)
-
-    for g in range(groups):
-
-        def drain(i, _, g=g):
-            d = distance(i)
-
+
+        def drain(d, _, g=g):
             @pl.when(me - d >= 0)
             def _():
                 q_copy(g, me - d, me).wait_send()
@@ -317,7 +342,7 @@
 
             return 0
 
-        lax.fori_loop(0, n - 1, drain, 0)
+        lax.fori_loop(1, n, drain, 0)
         for j in range(1, nh):
             a_copy(g, lax.rem(hd + j, nh), hd).wait_send()
 
@@ -377,7 +402,7 @@
                 collective_id=0, has_side_effects=True, vmem_limit_bytes=56 * 1024 * 1024
             ),
         )(
-            selected.reshape(heads, -1),
+            selected,
             queries.reshape(tiles, rows, heads * width),
             keys,
             values,

time: 83.8 us -> 82.3 us (0.982)
  Pallas kernels: 79.6 us -> 78.6 us
    pallas_call x1, Pallas kernels: 79.6 us -> 78.6 us  [local(): pl.pallas_call(functools.partial(kernel, (n, nh, heads, tiles, rows, widt...]
where the time goes in v3:
time: 82.3 us; the launch traced here: 81.9 us
  Pallas kernels  78.6 us (96%)
  local copies, waits for them, and re-layouts  3.3 us (4%)
    pallas_call x1, Pallas kernels, local(): pl.pallas_call(functools.partial(kernel, (n, nh, heads, tiles, rows, widt...  78.6 us
    unnamed x2, local copies, waits for them, and re-layouts  3.3 us

profile of v3, /device:TPU:16, one launch (start us, length us, event | category | flops | bytes accessed | tf_op | source)
XLA Modules:
  0.0 81.9 jit_solution(4572738782949542649)
XLA Ops:
  0.0 1.4 %copy.6.sel = s32[8,8,3]{2,1,0:T(8,128)} copy(s32[8,8,3]{1,0,2:T(8,128)} %param.8) | data formatting | bytes 1536 | tf_op args[3]
  1.4 78.6 %shard_map.55 = bf16[256,1024]{1,0:T(8,128)(2,1)} custom-call(s32[8,8,3]{2,1,0:T(8,128)} %copy.6.sel, bf16[8,32,1024]{2,1,0:T(8,128)(2,1)} %bitcast.3, bf16[256,1024]{1,0:T(8,128)(2,1)} %k_hbm.1, bf16[256,1024]{1,0:T(8,128)(2,1)} %v_hbm.1, bf16[2,4,256,1024]{3,2,1,0:T(8,128)(2,1)} %bitcast.2), custom_call_target="tpu_custom_call" | custom-call | tf_op jit(solution)/shard_map/pallas_call | solution.py:370
  80.0 1.9 %copy.8 = bf16[256,1024]{1,0:T(8,128)(2,1)} copy(bf16[256,1024]{1,0:T(8,128)(2,1)} %shard_map.55) | data formatting | bytes 1048576

commit v4 on v3

--- a/solution.py
+++ b/solution.py
@@ -8,7 +8,7 @@
 from jax.sharding import PartitionSpec as P
 
 CAP = 2
-AHEAD = 2
+AHEAD = 4
 LAG = 2
 TEAM = 4
 MESH = pl.DeviceIdType.MESH
@@ -28,31 +28,28 @@
 
 
 def fill_tables(n, tiles, sel, tblv):
-    heads, _, each = sel.shape
-    entries = tiles * each
+    each, heads, _ = sel.shape
+    entries = (each - 1) * tiles
     lane = lax.broadcasted_iota(jnp.int32, (heads, entries), 1)
     picks = jnp.zeros((heads, entries), jnp.int32)
+    tile_of = lane
     column = []
-    for t in range(tiles):
-        chosen = sel[:, t, :]
-        for r in range(each):
-            column.append(chosen[:, r : r + 1])
-            picks = jnp.where(lane == t * each + r, column[-1], picks)
-    tile_of = jnp.zeros((heads, entries), jnp.int32)
-    for t in range(1, tiles):
-        tile_of += jnp.where(lane >= t * each, 1, 0)
-    other = lane != tile_of * each
+    for r in range(1, each):
+        chosen = sel[r]
+        tile_of = jnp.where(lane >= (r - 1) * tiles, lane - (r - 1) * tiles, tile_of)
+        for t in range(tiles):
+            column.append(chosen[:, t : t + 1])
+            picks = jnp.where(lane == (r - 1) * tiles + t, column[-1], picks)
     rank = jnp.zeros((heads, entries), jnp.int32)
     for j in range(entries):
-        if j % each != 0:
-            rank += jnp.where((picks == column[j]) & (lane > j) & other, 1, 0)
+        rank += jnp.where((picks == column[j]) & (lane > j), 1, 0)
     slot = jnp.minimum(rank, CAP - 1)
     lanes = tblv.shape[2]
     wide = lax.broadcasted_iota(jnp.int32, (heads, lanes), 1)
     found = jnp.zeros((heads, lanes), jnp.int32)
     for a in range(n):
         for s in range(CAP):
-            hit = other & (picks == a) & (slot == s)
+            hit = (picks == a) & (slot == s)
             tile = jnp.max(jnp.where(hit, tile_of, 0), axis=1, keepdims=True)
             found = jnp.where(wide == a * CAP + s, tile, found)
     tblv[0] = found
@@ -204,12 +201,13 @@
     causal = lax.broadcasted_iota(jnp.int32, (tokens, tokens), 0) >= lax.broadcasted_iota(
         jnp.int32, (tokens, tokens), 1
     )
-    for h in range(heads):
-        cols = slice(h * width, (h + 1) * width)
-        query = q[:, :, cols].reshape(tokens, width)
-        part, lse = softmax_block(query, k[:, cols], v[:, cols], scale, causal)
-        own[h] = part.reshape(tiles, rows, width)
-        own_lse[h] = jnp.broadcast_to(lse, (tokens, width)).reshape(tiles, rows, width)
+    def own_group(g):
+        for h in range(g * per, (g + 1) * per):
+            cols = slice(h * width, (h + 1) * width)
+            query = q[:, :, cols].reshape(tokens, width)
+            part, lse = softmax_block(query, k[:, cols], v[:, cols], scale, causal)
+            own[h] = part.reshape(tiles, rows, width)
+            own_lse[h] = jnp.broadcast_to(lse, (tokens, width)).reshape(tiles, rows, width)
 
     short = CAP * rows
     stat_lanes = ssend.shape[3]
@@ -296,8 +294,8 @@
             h = g * per + hh
 
             def gather(r):
-                blocks = [tbl[1, h, t * 3 + r] for t in range(tiles)]
-                slots = [tbl[2, h, t * 3 + r] for t in range(tiles)]
+                blocks = [tbl[1, h, (r - 1) * tiles + t] for t in range(tiles)]
+                slots = [tbl[2, h, (r - 1) * tiles + t] for t in range(tiles)]
                 outs = [orecv[g][a, hh, s] for a, s in zip(blocks, slots)]
                 lses = [picked_lse(a, s, hh) for a, s in zip(blocks, slots)]
                 return jnp.concatenate(outs, 0).astype(jnp.float32), jnp.concatenate(lses, 0)
@@ -312,10 +310,13 @@
         for j in range(1, nh):
             a_copy(g, lax.rem(hd + j, nh), hd).start()
 
+    own_group(0)
     for g in range(groups):
         answer_group(g)
         if g + AHEAD < groups:
             send_group(g + AHEAD)
+        if g + 1 < groups:
+            own_group(g + 1)
         if g >= LAG:
             collect_group(g - LAG)
     for g in range(max(groups - LAG, 0), groups):
@@ -402,7 +403,7 @@
                 collective_id=0, has_side_effects=True, vmem_limit_bytes=56 * 1024 * 1024
             ),
         )(
-            selected,
+            jnp.transpose(selected, (2, 0, 1)),
             queries.reshape(tiles, rows, heads * width),
             keys,
             values,

time: 82.3 us -> 80.7 us (0.981)
  local copies, waits for them, and re-layouts: 3.3 us -> 1.87 us
    unnamed x2 -> x1, local copies, waits for them, and re-layouts: 3.3 us -> 1.87 us
where the time goes in v4:
time: 80.7 us; the launch traced here: 80.3 us
  Pallas kernels  78.4 us (97%)
  local copies, waits for them, and re-layouts  1.87 us (2%)
    pallas_call x1, Pallas kernels, local(): pl.pallas_call(functools.partial(kernel, (n, nh, heads, tiles, rows, widt...  78.4 us
    unnamed x1, local copies, waits for them, and re-layouts  1.87 us

profile of v4, /device:TPU:16, one launch (start us, length us, event | category | flops | bytes accessed | tf_op | source)
XLA Modules:
  0.0 80.3 jit_solution(7878672285784199235)
XLA Ops:
  0.0 78.4 %shard_map.55 = bf16[256,1024]{1,0:T(8,128)(2,1)} custom-call(s32[3,8,8]{2,1,0:T(8,128)} %bitcast.5, bf16[8,32,1024]{2,1,0:T(8,128)(2,1)} %bitcast.4, bf16[256,1024]{1,0:T(8,128)(2,1)} %k_hbm.1, bf16[256,1024]{1,0:T(8,128)(2,1)} %v_hbm.1, bf16[2,4,256,1024]{3,2,1,0:T(8,128)(2,1)} %bitcast.3), custom_call_target="tpu_custom_call" | custom-call | tf_op jit(solution)/shard_map/pallas_call | solution.py:371
  78.4 1.9 %copy.7 = bf16[256,1024]{1,0:T(8,128)(2,1)} copy(bf16[256,1024]{1,0:T(8,128)(2,1)} %shard_map.55) | data formatting | bytes 1048576

commit v5 on v4

--- a/solution.py
+++ b/solution.py
@@ -8,8 +8,8 @@
 from jax.sharding import PartitionSpec as P
 
 CAP = 2
-AHEAD = 4
-LAG = 2
+AHEAD = 2
+LAG = 1
 TEAM = 4
 MESH = pl.DeviceIdType.MESH
 LOG2E = 1.4426950408889634
@@ -24,7 +24,7 @@
     prob = jnp.exp2((scores - top) * (scale * LOG2E))
     total = jnp.sum(prob, axis=-1, keepdims=True)
     part = jnp.dot(prob.astype(jnp.bfloat16), value, preferred_element_type=jnp.float32)
-    return part * (1.0 / total), top * scale + jnp.log(total)
+    return part * (1.0 / total), top, total
 
 
 def fill_tables(n, tiles, sel, tblv):
@@ -205,14 +205,19 @@
         for h in range(g * per, (g + 1) * per):
             cols = slice(h * width, (h + 1) * width)
             query = q[:, :, cols].reshape(tokens, width)
-            part, lse = softmax_block(query, k[:, cols], v[:, cols], scale, causal)
+            part, top, total = softmax_block(query, k[:, cols], v[:, cols], scale, causal)
+            lse = top * scale + jnp.log(total)
             own[h] = part.reshape(tiles, rows, width)
             own_lse[h] = jnp.broadcast_to(lse, (tokens, width)).reshape(tiles, rows, width)
 
     short = CAP * rows
     stat_lanes = ssend.shape[3]
-    lane = lax.broadcasted_iota(jnp.int32, (TEAM, short, stat_lanes), 2)
-    lane = lane - lax.broadcasted_iota(jnp.int32, (TEAM, short, stat_lanes), 1)
+    lane = lax.broadcasted_iota(jnp.int32, (TEAM, short, 128), 2)
+    lane = lane - lax.broadcasted_iota(jnp.int32, (TEAM, short, 128), 1)
+
+    def as_row(hit, column):
+        column = jnp.broadcast_to(column, (TEAM * short, 128)).reshape(TEAM, short, 128)
+        return jnp.sum(jnp.where(hit, column, 0.0), axis=1, keepdims=True)
 
     def answer_group(g):
         orecv[g][me] = jnp.zeros((per, CAP, rows, width), jnp.bfloat16)
@@ -231,17 +236,23 @@
                         q_copy(g, me, there).wait_recv()
 
                 team = pl.ds(pl.multiple_of(their * TEAM, TEAM), TEAM)
-                stats = jnp.zeros((TEAM, short, stat_lanes), jnp.float32)
-                for hh in range(per):
-                    h = g * per + hh
-                    cols = slice(h * width, (h + 1) * width)
-                    query = qrecv[g][team, hh].reshape(TEAM * short, width)
-                    part, lse = softmax_block(query, k[:, cols], v[:, cols], scale, None)
-                    osend[g, team, hh] = part.astype(jnp.bfloat16).reshape(TEAM, CAP, rows, width)
-                    lse = jnp.broadcast_to(lse, (TEAM * short, stat_lanes))
-                    lse = lse.reshape(TEAM, short, stat_lanes)
-                    stats = jnp.where(lane == hh * short, lse, stats)
-                ssend[g, team] = jnp.sum(stats, axis=1, keepdims=True)
+                both = 128 // short
+                for first in range(0, per, both):
+                    tops = jnp.zeros((TEAM, 1, 128), jnp.float32)
+                    totals = jnp.zeros((TEAM, 1, 128), jnp.float32)
+                    for hh in range(first, min(first + both, per)):
+                        h = g * per + hh
+                        cols = slice(h * width, (h + 1) * width)
+                        query = qrecv[g][team, hh].reshape(TEAM * short, width)
+                        part, top, total = softmax_block(query, k[:, cols], v[:, cols], scale, None)
+                        part = part.astype(jnp.bfloat16).reshape(TEAM, CAP, rows, width)
+                        osend[g, team, hh] = part
+                        hit = lane == (hh - first) * short
+                        tops += as_row(hit, top)
+                        totals += as_row(hit, total)
+                    ssend[g, team, :, first * short : first * short + 128] = tops * scale + jnp.log(
+                        totals
+                    )
                 for j in range(TEAM):
                     there = member(their, j)
 
@@ -270,8 +281,8 @@
 
         lax.fori_loop(0, out_ref.shape[1] // part_cols, body, 0)
 
-    lane_tile = lax.broadcasted_iota(jnp.int32, (rows, stat_lanes), 1)
-    lane_tile = lane_tile - lax.broadcasted_iota(jnp.int32, (rows, stat_lanes), 0)
+    lane_tile = lax.broadcasted_iota(jnp.int32, (rows, 128), 1)
+    lane_tile = lane_tile - lax.broadcasted_iota(jnp.int32, (rows, 128), 0)
 
     def collect_group(g):
         def collect(i, _):
@@ -287,8 +298,10 @@
         lax.fori_loop(0, n, collect, 0)
 
         def picked_lse(block, slot, hh):
-            hit = lane_tile == hh * short + slot * rows
-            return jnp.sum(jnp.where(hit, srecv[g][block], 0.0), axis=1, keepdims=True)
+            at = hh * short // 128 * 128
+            hit = lane_tile == hh * short - at + slot * rows
+            row = srecv[g][block][:, at : at + 128]
+            return jnp.sum(jnp.where(hit, row, 0.0), axis=1, keepdims=True)
 
         for hh in range(per):
             h = g * per + hh
@@ -323,6 +336,22 @@
         collect_group(g)
     loads[3].wait()
     project(hd, nh == 1)
+    for g in range(groups):
+
+        def drain(d, _, g=g):
+            @pl.when(me - d >= 0)
+            def _():
+                q_copy(g, me - d, me).wait_send()
+
+            @pl.when(me + d < n)
+            def _():
+                o_copy(g, me + d, me).wait_send()
+                s_copy(g, me + d, me).wait_send()
+
+            return 0
+
+        lax.fori_loop(1, n, drain, 0)
+
     for j in range(1, nh):
         peer = lax.rem(hd + j, nh)
         for g in range(groups):
@@ -330,20 +359,6 @@
         project(peer, j == nh - 1)
 
     for g in range(groups):
-
-        def drain(d, _, g=g):
-            @pl.when(me - d >= 0)
-            def _():
-                q_copy(g, me - d, me).wait_send()
-
-            @pl.when(me + d < n)
-            def _():
-                o_copy(g, me + d, me).wait_send()
-                s_copy(g, me + d, me).wait_send()
-
-            return 0
-
-        lax.fori_loop(1, n, drain, 0)
         for j in range(1, nh):
             a_copy(g, lax.rem(hd + j, nh), hd).wait_send()
 
@@ -356,7 +371,7 @@
         tokens, cols = queries.shape[0], out_weight.shape[1]
         width = queries.shape[1] // heads
         rows = tokens // tiles
-        per = 2 if heads % 2 == 0 and heads >= 4 else 1
+        per = 4 if heads % 4 == 0 else 1
         groups = heads // per
         stat_lanes = -(-per * CAP * rows // 128) * 128
         table = (3, heads, -(-max(n * CAP, tiles * 3) // 128) * 128)

time: 80.7 us -> 85.8 us (1.063)
  the two profiles are of different devices: /device:TPU:16 before, /device:TPU:19 now
where the time goes in v5:
time: 85.8 us; the launch traced here: 85.6 us
  Pallas kernels  83.7 us (98%)
  local copies, waits for them, and re-layouts  1.87 us (2%)
    pallas_call x1, Pallas kernels, local(): pl.pallas_call(functools.partial(kernel, (n, nh, heads, tiles, rows, widt...  83.7 us
    unnamed x1, local copies, waits for them, and re-layouts  1.87 us

profile of v5, /device:TPU:19, one launch (start us, length us, event | category | flops | bytes accessed | tf_op | source)
XLA Modules:
  0.0 85.6 jit_solution(5465184241370438160)
XLA Ops:
  0.0 83.7 %shard_map.55 = bf16[256,1024]{1,0:T(8,128)(2,1)} custom-call(s32[3,8,8]{2,1,0:T(8,128)} %bitcast.5, bf16[8,32,1024]{2,1,0:T(8,128)(2,1)} %bitcast.4, bf16[256,1024]{1,0:T(8,128)(2,1)} %k_hbm.1, bf16[256,1024]{1,0:T(8,128)(2,1)} %v_hbm.1, bf16[2,2,512,1024]{3,2,1,0:T(8,128)(2,1)} %bitcast.3), custom_call_target="tpu_custom_call" | custom-call | tf_op jit(solution)/shard_map/pallas_call | solution.py:386
  83.7 1.9 %copy.7 = bf16[256,1024]{1,0:T(8,128)(2,1)} copy(bf16[256,1024]{1,0:T(8,128)(2,1)} %shard_map.55) | data formatting | bytes 1048576

commit v6 on v5

--- a/solution.py
+++ b/solution.py
@@ -8,8 +8,8 @@
 from jax.sharding import PartitionSpec as P
 
 CAP = 2
-AHEAD = 2
-LAG = 1
+AHEAD = 4
+LAG = 2
 TEAM = 4
 MESH = pl.DeviceIdType.MESH
 LOG2E = 1.4426950408889634
@@ -371,7 +371,7 @@
         tokens, cols = queries.shape[0], out_weight.shape[1]
         width = queries.shape[1] // heads
         rows = tokens // tiles
-        per = 4 if heads % 4 == 0 else 1
+        per = 1
         groups = heads // per
         stat_lanes = -(-per * CAP * rows // 128) * 128
         table = (3, heads, -(-max(n * CAP, tiles * 3) // 128) * 128)

time: 85.8 us -> 83 us (0.967)
  the two profiles are of different devices: /device:TPU:19 before, /device:TPU:16 now
where the time goes in v6:
time: 83 us; the launch traced here: 82.7 us
  Pallas kernels  80.8 us (97%)
  local copies, waits for them, and re-layouts  1.87 us (2%)
    pallas_call x1, Pallas kernels, local(): pl.pallas_call(functools.partial(kernel, (n, nh, heads, tiles, rows, widt...  80.8 us
    unnamed x1, local copies, waits for them, and re-layouts  1.87 us

profile of v6, /device:TPU:16, one launch (start us, length us, event | category | flops | bytes accessed | tf_op | source)
XLA Modules:
  0.0 82.7 jit_solution(7806784087706784720)
XLA Ops:
  0.0 80.8 %shard_map.55 = bf16[256,1024]{1,0:T(8,128)(2,1)} custom-call(s32[3,8,8]{2,1,0:T(8,128)} %bitcast.5, bf16[8,32,1024]{2,1,0:T(8,128)(2,1)} %bitcast.4, bf16[256,1024]{1,0:T(8,128)(2,1)} %k_hbm.1, bf16[256,1024]{1,0:T(8,128)(2,1)} %v_hbm.1, bf16[2,8,128,1024]{3,2,1,0:T(8,128)(2,1)} %bitcast.3), custom_call_target="tpu_custom_call" | custom-call | tf_op jit(solution)/shard_map/pallas_call | solution.py:386
  80.8 1.9 %copy.7 = bf16[256,1024]{1,0:T(8,128)(2,1)} copy(bf16[256,1024]{1,0:T(8,128)(2,1)} %shard_map.55) | data formatting | bytes 1048576

commit v7 on v5

--- a/solution.py
+++ b/solution.py
@@ -8,7 +8,6 @@
 from jax.sharding import PartitionSpec as P
 
 CAP = 2
-AHEAD = 2
 LAG = 1
 TEAM = 4
 MESH = pl.DeviceIdType.MESH
@@ -194,7 +193,7 @@
 
         lax.fori_loop(0, n, send_queries, 0)
 
-    for g in range(min(AHEAD, groups)):
+    for g in range(groups):
         send_group(g)
     loads[1].wait()
     loads[2].wait()
@@ -219,14 +218,13 @@
         column = jnp.broadcast_to(column, (TEAM * short, 128)).reshape(TEAM, short, 128)
         return jnp.sum(jnp.where(hit, column, 0.0), axis=1, keepdims=True)
 
-    def answer_group(g):
+    def clear_group(g):
         orecv[g][me] = jnp.zeros((per, CAP, rows, width), jnp.bfloat16)
         srecv[g][me] = jnp.full((1, stat_lanes), -1e30, jnp.float32)
 
-        def answer(i, _):
-            their = level + distance(i)
-
-            @pl.when(their < levels)
+    def answer_team(g, their, wanted):
+        def answer():
+            @pl.when(wanted)
             def _():
                 for j in range(TEAM):
                     there = member(their, j)
@@ -261,9 +259,7 @@
                         o_copy(g, there, me).start()
                         s_copy(g, there, me).start()
 
-            return 0
-
-        lax.fori_loop(0, levels, answer, 0)
+        answer()
 
     part_cols = min(256, out_ref.shape[1])
 
@@ -323,13 +319,25 @@
         for j in range(1, nh):
             a_copy(g, lax.rem(hd + j, nh), hd).start()
 
-    own_group(0)
+    top_level = levels - 1
     for g in range(groups):
-        answer_group(g)
-        if g + AHEAD < groups:
-            send_group(g + AHEAD)
-        if g + 1 < groups:
-            own_group(g + 1)
+        clear_group(g)
+
+        def answer_between(i, _, g=g):
+            their = level + distance(i)
+            answer_team(g, their, (their > level) & (their < top_level))
+            return 0
+
+        lax.fori_loop(0, levels, answer_between, 0)
+        own_group(g)
+    for g in range(groups):
+
+        def answer_rest(i, _, g=g):
+            their = jnp.where(i == 0, top_level, level)
+            answer_team(g, their, (i == 1) | (their > level))
+            return 0
+
+        lax.fori_loop(0, 2, answer_rest, 0)
         if g >= LAG:
             collect_group(g - LAG)
     for g in range(max(groups - LAG, 0), groups):
@@ -371,7 +379,7 @@
         tokens, cols = queries.shape[0], out_weight.shape[1]
         width = queries.shape[1] // heads
         rows = tokens // tiles
-        per = 4 if heads % 4 == 0 else 1
+        per = 2 if heads % 4 == 0 else 1
         groups = heads // per
         stat_lanes = -(-per * CAP * rows // 128) * 128
         table = (3, heads, -(-max(n * CAP, tiles * 3) // 128) * 128)

time: 85.8 us -> 93.9 us (1.094)
  the two profiles are of different devices: /device:TPU:19 before, /device:TPU:25 now
where the time goes in v7:
time: 93.9 us; the launch traced here: 93.7 us
  Pallas kernels  91.8 us (98%)
  local copies, waits for them, and re-layouts  1.87 us (2%)
    pallas_call x1, Pallas kernels, local(): pl.pallas_call(functools.partial(kernel, (n, nh, heads, tiles, rows, widt...  91.8 us

profile of v7, /device:TPU:25, one launch (start us, length us, event | category | flops | bytes accessed | tf_op | source)
XLA Modules:
  0.0 93.7 jit_solution(826230613708123995)
XLA Ops:
  0.0 91.8 %shard_map.55 = bf16[256,1024]{1,0:T(8,128)(2,1)} custom-call(s32[3,8,8]{2,1,0:T(8,128)} %bitcast.5, bf16[8,32,1024]{2,1,0:T(8,128)(2,1)} %bitcast.4, bf16[256,1024]{1,0:T(8,128)(2,1)} %k_hbm.1, bf16[256,1024]{1,0:T(8,128)(2,1)} %v_hbm.1, bf16[2,4,256,1024]{3,2,1,0:T(8,128)(2,1)} %bitcast.3), custom_call_target="tpu_custom_call" | custom-call | tf_op jit(solution)/shard_map/pallas_call | solution.py:394
  91.8 1.9 %copy.7 = bf16[256,1024]{1,0:T(8,128)(2,1)} copy(bf16[256,1024]{1,0:T(8,128)(2,1)} %shard_map.55) | data formatting | bytes 1048576

commit v8 on v6

--- a/solution.py
+++ b/solution.py
@@ -125,7 +125,7 @@
 
     def distance(i):
         half = (i + 1) // 2
-        return levels // 2 + jnp.where(i % 2 == 0, half, -half)
+        return levels // 2 + jnp.where(i % 2 == 0, -half, half)
 
     def member(at_level, j):
         return at_level * TEAM + lax.rem(place + j, TEAM)
@@ -192,7 +192,7 @@
 
             return 0
 
-        lax.fori_loop(0, n, send_queries, 0)
+        lax.fori_loop(0, n + TEAM, send_queries, 0)
 
     for g in range(min(AHEAD, groups)):
         send_group(g)
@@ -263,7 +263,7 @@
 
             return 0
 
-        lax.fori_loop(0, levels, answer, 0)
+        lax.fori_loop(0, levels + 1, answer, 0)
 
     part_cols = min(256, out_ref.shape[1])
 
@@ -295,7 +295,7 @@
 
             return 0
 
-        lax.fori_loop(0, n, collect, 0)
+        lax.fori_loop(0, n + TEAM, collect, 0)
 
         def picked_lse(block, slot, hh):
             at = hh * short // 128 * 128
@@ -371,7 +371,7 @@
         tokens, cols = queries.shape[0], out_weight.shape[1]
         width = queries.shape[1] // heads
         rows = tokens // tiles
-        per = 1
+        per = 2 if heads % 4 == 0 else 1
         groups = heads // per
         stat_lanes = -(-per * CAP * rows // 128) * 128
         table = (3, heads, -(-max(n * CAP, tiles * 3) // 128) * 128)

time: 83 us -> 81.4 us (0.981)
  Pallas kernels: 80.8 us -> 79.3 us
    pallas_call x1, Pallas kernels: 80.8 us -> 79.3 us  [local(): pl.pallas_call(functools.partial(kernel, (n, nh, heads, tiles, rows, widt...]
where the time goes in v8:
time: 81.4 us; the launch traced here: 81.2 us
  Pallas kernels  79.3 us (97%)
  local copies, waits for them, and re-layouts  1.87 us (2%)
    pallas_call x1, Pallas kernels, local(): pl.pallas_call(functools.partial(kernel, (n, nh, heads, tiles, rows, widt...  79.3 us
    unnamed x1, local copies, waits for them, and re-layouts  1.87 us

profile of v8, /device:TPU:16, one launch (start us, length us, event | category | flops | bytes accessed | tf_op | source)
XLA Modules:
  0.0 81.2 jit_solution(14954429521785592069)
XLA Ops:
  0.0 79.3 %shard_map.55 = bf16[256,1024]{1,0:T(8,128)(2,1)} custom-call(s32[3,8,8]{2,1,0:T(8,128)} %bitcast.5, bf16[8,32,1024]{2,1,0:T(8,128)(2,1)} %bitcast.4, bf16[256,1024]{1,0:T(8,128)(2,1)} %k_hbm.1, bf16[256,1024]{1,0:T(8,128)(2,1)} %v_hbm.1, bf16[2,4,256,1024]{3,2,1,0:T(8,128)(2,1)} %bitcast.3), custom_call_target="tpu_custom_call" | custom-call | tf_op jit(solution)/shard_map/pallas_call | solution.py:386
  79.3 1.9 %copy.7 = bf16[256,1024]{1,0:T(8,128)(2,1)} copy(bf16[256,1024]{1,0:T(8,128)(2,1)} %shard_map.55) | data formatting | bytes 1048576
